TPU v7x, 32 devices: a whole 2x2x4 slice. The times are simulated.
32 devices in a mesh: grp: 2 (over x), gy: 8 (over z, y), ch: 2 (over core).
Axes of the slice: x: 2, y: 2, z: 4, core: 2. Of those that a mesh axis runs over, the one named last changes fastest.
Arguments:
- inputs: bfloat16 [256, 8, 16, 256], P(None, 'gy', 'grp'), parts along dimension 2, may hold values from -6 to 6
- cotangent: bfloat16 [256, 8, 16, 256], P('ch', 'gy', 'grp'), parts along dimension 2, may hold values from -6 to 6
- weight: bfloat16 [27, 256, 256], P(None, None, 'ch'), may hold values from -0.078125 to 0.078125
Outputs:
- input_grad: bfloat16 [256, 8, 16, 256], P('ch', 'gy', 'grp'), parts along dimension 2
- weight_grad: float32 [54, 256, 256], P('grp', None, 'ch'), parts along dimension 0
There are 2 independent parts, one for each index of `grp`. A program takes and returns all parts, laid end to end along the dimension named above; an argument that names none is the same for every part. Nothing has to cross between parts.
All inputs are finite; a program needn't handle non-finite values.
Results may differ from a plain program's by a relative error of at most 0.0013.
Values may be sent and summed in bfloat16 or wider, within the bound.
A program may use at most 192 MiB of HBM per device.

v0:
```python
import math
import jax
import jax.numpy as jnp
from jax import lax
from jax.sharding import PartitionSpec as P


def padded(block, sides, width):
    for axis, dim in sides:
        count = lax.axis_size(axis)
        forward = [(i, i + 1) for i in range(count - 1)]
        backward = [(target, source) for source, target in forward]
        low = lax.ppermute(
            lax.slice_in_dim(block, block.shape[dim] - width, None, axis=dim), axis, forward
        )
        high = lax.ppermute(lax.slice_in_dim(block, 0, width, axis=dim), axis, backward)
        block = jnp.concatenate([low, block, high], axis=dim)
    return block


def shift_cells(flat, z_step, x_step, x_count):
    offset = z_step * x_count + x_step
    length = flat.shape[-1]
    if offset > 0:
        filler = jnp.zeros(flat.shape[:-1] + (offset,), flat.dtype)
        moved = jnp.concatenate([filler, flat[..., : length - offset]], axis=-1)
    elif offset < 0:
        filler = jnp.zeros(flat.shape[:-1] + (-offset,), flat.dtype)
        moved = jnp.concatenate([flat[..., -offset:], filler], axis=-1)
    else:
        moved = flat
    if x_step == 0:
        return moved
    column = jnp.arange(length) % x_count - x_step
    keep = (column >= 0) & (column < x_count)
    return jnp.where(keep, moved, jnp.zeros((), flat.dtype))


def grad_group(planes, y_off, x_count):
    row_count = planes.shape[1] - 2
    flat = planes.reshape(planes.shape[0], planes.shape[1], -1)
    window = flat[:, 2 - y_off : 2 - y_off + row_count, :]
    pieces_list = []
    for z_off in range(3):
        for x_off in range(3):
            pieces_list.append(shift_cells(window, z_off - 1, x_off - 1, x_count))
    stacked = jnp.stack(pieces_list, 0)
    return stacked.reshape(9 * planes.shape[0], -1)


def local(inputs, cotangent, weight):
    channel_count = inputs.shape[0]
    local_out = cotangent.shape[0]
    row_count = inputs.shape[1]
    z_count = inputs.shape[2]
    x_count = inputs.shape[3]
    cell_count = row_count * z_count * x_count
    owned_rows = channel_count // lax.axis_size("ch")
    weight_rows = jnp.transpose(weight, (1, 0, 2))
    planes = padded(cotangent, (("gy", 1),), 1)
    stacks = []
    stacks = [grad_group(planes, y_off, x_count) for y_off in range(3)]
    summed = jnp.zeros((owned_rows * lax.axis_size("ch"), cell_count), jnp.float32)
    for partial_y_off in range(3):
        tap_cols = weight_rows[:, 9 * partial_y_off : 9 * partial_y_off + 9, :].reshape(
            owned_rows * lax.axis_size("ch"), -1
        )
        summed = summed + jnp.dot(
            tap_cols, stacks[partial_y_off], preferred_element_type=jnp.float32
        )
    grad_rows = lax.psum_scatter(summed, "ch", scatter_dimension=0, tiled=True)
    input_grad = grad_rows.astype(jnp.bfloat16).reshape(owned_rows, row_count, z_count, x_count)
    tap_grads = []
    input_halo = padded(inputs, (("gy", 1),), 1)
    halo_flat = input_halo.reshape(channel_count, row_count + 2, -1)
    grad_flat = cotangent.reshape(local_out, -1)
    for y_off in range(3):
        window = halo_flat[:, y_off : y_off + row_count, :]
        for z_off in range(3):
            for x_off in range(3):
                moved = shift_cells(window, 1 - z_off, 1 - x_off, x_count).reshape(
                    channel_count, -1
                )
                tap_grads.append(
                    lax.dot_general(
                        moved,
                        grad_flat,
                        (((1,), (1,)), ((), ())),
                        preferred_element_type=jnp.float32,
                    )
                )
    local_grad = jnp.stack(tap_grads, 0)
    norm_factor = 1.0 / math.sqrt(row_count * lax.axis_size("gy") * z_count * x_count)
    weight_grad = lax.psum(local_grad, "gy") * norm_factor
    return (input_grad, weight_grad)


def solution(mesh):
    placed = (P(None, "gy", "grp", None), P("ch", "gy", "grp", None), P(None, None, "ch"))
    return jax.shard_map(
        local,
        mesh=mesh,
        in_specs=placed,
        out_specs=(P("ch", "gy", "grp", None), P("grp", None, "ch")),
        check_vma=False,
    )
```

profile of v0, /device:TPU:0, one launch (start us, length us, event | category | flops | bytes accessed | tf_op | source)
XLA Modules:
  0.0 311.7 jit_solution(372415313402467962)
XLA Ops:
  8.1 2.3 copy.71
  11.6 6.3 %collective-permute-start = (bf16[128,1,8,256]{0,3,2,1:T(8,128)(2,1)}, bf16[128,1,8,256]{0,3,2,1:T(8,128)(2,1)}, u32[]{:S(2)}, u32[]{:S(2)}) collective-permute-start(bf16[128,1,8,256]{0,3,2,1:T(8,128)(2,1)} %copy.71), channel_id=1, source_target_pairs={{0,2},{2,4},{4,6},{6,8},{8,10},{10,12},{12,14},{1,3},{3,5},{5,7},{... | collective-permute-start | bytes 1572872 | tf_op jit(solution)/shard_map/ppermute | solution.py:13
  17.9 1.6 copy.80
  20.9 5.6 %collective-permute-start.2 = (bf16[256,1,8,256]{0,3,2,1:T(8,128)(2,1)S(1)}, bf16[256,1,8,256]{0,3,2,1:T(8,128)(2,1)}, u32[]{:S(2)}, u32[]{:S(2)}) collective-permute-start(bf16[256,1,8,256]{0,3,2,1:T(8,128)(2,1)S(1)} %copy.80), channel_id=1, source_target_pairs={{0,2},{2,4},{4,6},{6,8},{8,10},{10,12},{12,14},{1,3},{3,5},{5,7},{... | collective-permute-start | bytes 3145736 | tf_op jit(solution)/shard_map/ppermute | solution.py:13
  26.5 2.6 copy.75
  31.4 30.0 %collective-permute-done = bf16[128,1,8,256]{0,3,2,1:T(8,128)(2,1)} collective-permute-done((bf16[128,1,8,256]{0,3,2,1:T(8,128)(2,1)}, bf16[128,1,8,256]{0,3,2,1:T(8,128)(2,1)}, u32[]{:S(2)}, u32[]{:S(2)}) %collective-permute-start) | collective-permute-done | bytes 524320 | tf_op jit(solution)/shard_map/ppermute | solution.py:13
  61.4 1.5 pad_maximum_fusion.1
  66.6 1.6 fusion.164
  72.8 2.7 copy-done.4
  75.5 8.2 %collective-permute-done.2 = bf16[256,1,8,256]{0,3,2,1:T(8,128)(2,1)} collective-permute-done((bf16[256,1,8,256]{0,3,2,1:T(8,128)(2,1)S(1)}, bf16[256,1,8,256]{0,3,2,1:T(8,128)(2,1)}, u32[]{:S(2)}, u32[]{:S(2)}) %collective-permute-start.2) | collective-permute-done | bytes 1048608 | tf_op jit(solution)/shard_map/ppermute | solution.py:13
  83.7 1.9 pad_maximum_fusion
  85.5 2.6 fusion.156
  88.1 2.5 fusion.157
  90.6 2.7 fusion.158
  93.4 3.0 fusion.159
  96.4 2.2 copy.112
  98.6 3.0 fusion.27
  101.6 2.4 fusion.26
  105.5 1.5 fusion.24
  108.2 2.2 copy.113
  110.4 2.2 copy.114
  112.6 3.0 fusion.22
  115.6 3.0 fusion.21
  119.7 1.5 fusion.19
  121.2 1.5 fusion.18
  123.8 1.5 fusion.16
  125.3 1.5 fusion.15
  128.0 2.2 copy.115
  130.2 2.2 copy.116
  132.4 3.0 fusion.13
  135.4 3.0 fusion.12
  139.5 1.5 fusion.10
  141.0 1.5 fusion.9
  145.1 1.5 fusion.6
  147.8 1.8 copy.117
  149.6 2.9 fusion.4
  152.5 1.6 fusion.3
  157.6 2.7 bitcast_dynamic-update-slice_fusion
  160.3 1.6 bitcast_dynamic-update-slice_fusion.10
  163.6 1.6 bitcast_dynamic-update-slice_fusion.8
  165.2 6.6 %copy.74 = bf16[9,128,1,2048]{3,1,0,2:T(8,128)(2,1)} copy(bf16[9,128,1,2048]{1,3,2,0:T(8,128)(2,1)} %get-tuple-element.73) | data formatting | bytes 9437184 | tf_op jit(solution)/shard_map/stack | solution.py:47
  171.8 6.7 %copy.76 = bf16[9,128,1,2048]{3,1,0,2:T(8,128)(2,1)} copy(bf16[9,128,1,2048]{1,3,2,0:T(8,128)(2,1)} %get-tuple-element.72) | data formatting | bytes 9437184 | tf_op jit(solution)/shard_map/stack | solution.py:47
  178.5 6.9 %copy.79 = bf16[9,128,1,2048]{3,1,0,2:T(8,128)(2,1)} copy(bf16[9,128,1,2048]{1,3,2,0:T(8,128)(2,1)} %get-tuple-element.62) | data formatting | bytes 9437184 | tf_op jit(solution)/shard_map/stack | solution.py:47
  185.4 4.2 %fusion.165 = f32[2048,256]{1,0:T(8,128)S(1)} fusion(bf16[1152,2048]{1,0:T(8,128)(2,1)} %bitcast.359, bf16[256,1152]{0,1:T(8,128)(2,1)S(1)} %bitcast.367), kind=kOutput, calls=%fused_computation.235 | convolution fusion | flops 1207959552 | bytes 7405568 | tf_op jit(solution)/shard_map/dot_general | solution.py:68
  189.6 1.7 convolution_add_fusion.1
  192.2 3.0 fusion
  195.3 102.3 %all-reduce.50.cloned.1.call-done = f32[27,256,128]{2,1,0:T(8,128)} async-done(((f32[27,256,128]{2,1,0:T(8,128)}), f32[27,256,128]{2,1,0:T(8,128)}) %all-reduce.50.cloned.1.call-update) | async-done | bytes 3538960 | tf_op jit(solution)/shard_map/psum | solution.py:94
  297.6 4.2 %broadcast_multiply_fusion = f32[27,256,128]{2,1,0:T(8,128)} fusion(f32[27,256,128]{2,1,0:T(8,128)} %all-reduce.50.cloned.1.call-done), kind=kLoop, calls=%fused_computation.4 | loop fusion | flops 884736 | bytes 7077888 | tf_op jit(solution)/shard_map/mul | solution.py:94
  (124 shorter events, 32.4 us)
Async XLA Ops:
  8.0 21.2 %copy-start.14 = (bf16[128,1,8,256]{3,2,1,0:T(8,128)(2,1)S(1)}, bf16[128,1,8,256]{3,2,1,0:T(8,128)(2,1)}, u32[]{:S(2)}) copy-start(bf16[128,1,8,256]{3,2,1,0:T(8,128)(2,1)} %param.4) | copy-start | bytes 1572868
  8.0 289.6 %all-reduce.50.cloned.1.call-start = ((), (), s32[]{:S(2)}) async-start(), calls=%async_computation.2 | async-start | bytes 7077888 | tf_op jit(solution)/shard_map/psum | solution.py:94
  10.3 21.0 %collective-permute-start.1 = (bf16[128,1,8,256]{0,3,2,1:T(8,128)(2,1)}, bf16[128,1,8,256]{0,3,2,1:T(8,128)(2,1)}, u32[]{:S(2)}, u32[]{:S(2)}) collective-permute-start(bf16[128,1,8,256]{0,3,2,1:T(8,128)(2,1)} %copy.71), channel_id=1, source_target_pairs={{2,0},{4,2},{6,4},{8,6},{10,8},{12,10},{14,12},{3,1},{5,3},{7,5},{... | collective-permute-start | bytes 1572872 | tf_op jit(solution)/shard_map/ppermute | solution.py:16
  11.6 49.8 %collective-permute-start = (bf16[128,1,8,256]{0,3,2,1:T(8,128)(2,1)}, bf16[128,1,8,256]{0,3,2,1:T(8,128)(2,1)}, u32[]{:S(2)}, u32[]{:S(2)}) collective-permute-start(bf16[128,1,8,256]{0,3,2,1:T(8,128)(2,1)} %copy.71), channel_id=1, source_target_pairs={{0,2},{2,4},{4,6},{6,8},{8,10},{10,12},{12,14},{1,3},{3,5},{5,7},{... | collective-permute-start | bytes 1572872 | tf_op jit(solution)/shard_map/ppermute | solution.py:13
  19.6 11.8 %copy-start.8 = (bf16[256,1,8,256]{0,3,2,1:T(8,128)(2,1)}, bf16[256,1,8,256]{0,3,2,1:T(8,128)(2,1)S(1)}, u32[]{:S(2)}) copy-start(bf16[256,1,8,256]{0,3,2,1:T(8,128)(2,1)S(1)} %copy.80) | copy-start | bytes 3145732
  19.6 53.2 %collective-permute-start.3 = (bf16[256,1,8,256]{0,3,2,1:T(8,128)(2,1)S(1)}, bf16[256,1,8,256]{0,3,2,1:T(8,128)(2,1)}, u32[]{:S(2)}, u32[]{:S(2)}) collective-permute-start(bf16[256,1,8,256]{0,3,2,1:T(8,128)(2,1)S(1)} %copy.80), channel_id=1, source_target_pairs={{2,0},{4,2},{6,4},{8,6},{10,8},{12,10},{14,12},{3,1},{5,3},{7,5},{... | collective-permute-start | bytes 3145736 | tf_op jit(solution)/shard_map/ppermute | solution.py:16
  20.9 62.8 %collective-permute-start.2 = (bf16[256,1,8,256]{0,3,2,1:T(8,128)(2,1)S(1)}, bf16[256,1,8,256]{0,3,2,1:T(8,128)(2,1)}, u32[]{:S(2)}, u32[]{:S(2)}) collective-permute-start(bf16[256,1,8,256]{0,3,2,1:T(8,128)(2,1)S(1)} %copy.80), channel_id=1, source_target_pairs={{0,2},{2,4},{4,6},{6,8},{8,10},{10,12},{12,14},{1,3},{3,5},{5,7},{... | collective-permute-start | bytes 3145736 | tf_op jit(solution)/shard_map/ppermute | solution.py:13
  70.8 12.8 %copy-start.9 = (bf16[256,1,8,256]{0,3,2,1:T(8,128)(2,1)S(1)}, bf16[256,1,8,256]{0,3,2,1:T(8,128)(2,1)}, u32[]{:S(2)}) copy-start(bf16[256,1,8,256]{0,3,2,1:T(8,128)(2,1)} %copy-done.8) | copy-start | bytes 3145732
  71.9 3.6 %copy-start.4 = (bf16[9,128,1,2048]{1,3,2,0:T(8,128)(2,1)}, bf16[9,128,1,2048]{1,3,2,0:T(8,128)(2,1)S(1)}, u32[]{:S(2)}) copy-start(bf16[9,128,1,2048]{1,3,2,0:T(8,128)(2,1)S(1)} %get-tuple-element.60) | copy-start | bytes 14155780
  71.9 11.8 %copy-start.6 = (bf16[9,128,1,2048]{1,3,2,0:T(8,128)(2,1)}, bf16[9,128,1,2048]{1,3,2,0:T(8,128)(2,1)S(1)}, u32[]{:S(2)}) copy-start(bf16[9,128,1,2048]{1,3,2,0:T(8,128)(2,1)S(1)} %get-tuple-element.61) | copy-start | bytes 14155780
  72.8 2.7 copy-start.5
  98.6 5.4 %copy-start = (bf16[16,8,8,256]{3,1,2,0:T(8,128)(2,1)S(1)}, bf16[16,8,8,256]{3,1,2,0:T(8,128)(2,1)}, u32[]{:S(2)}) copy-start(bf16[16,8,8,256]{3,1,2,0:T(8,128)(2,1)} %copy.118) | copy-start | bytes 1572868
  98.6 5.4 %copy-start.30 = (bf16[256,1,1793]{0,2,1:T(8,128)(2,1)S(1)}, bf16[256,1,1793]{0,2,1:T(8,128)(2,1)}, u32[]{:S(2)}) copy-start(bf16[256,1,1793]{0,2,1:T(8,128)(2,1)} %get-tuple-element.25) | copy-start | bytes 2754052
  98.6 6.9 %copy-start.26 = (bf16[256,1,2047]{0,2,1:T(8,128)(2,1)S(1)}, bf16[256,1,2047]{0,2,1:T(8,128)(2,1)}, u32[]{:S(2)}) copy-start(bf16[256,1,2047]{0,2,1:T(8,128)(2,1)} %get-tuple-element.31) | copy-start | bytes 3144196
  112.6 6.0 %copy-start.1 = (bf16[16,8,8,256]{3,1,2,0:T(8,128)(2,1)S(1)}, bf16[16,8,8,256]{3,1,2,0:T(8,128)(2,1)}, u32[]{:S(2)}) copy-start(bf16[16,8,8,256]{3,1,2,0:T(8,128)(2,1)} %copy.118) | copy-start | bytes 1572868
  112.6 6.0 %copy-start.12 = (bf16[256,1,1792]{2,0,1:T(8,128)(2,1)S(1)}, bf16[256,1,1792]{2,0,1:T(8,128)(2,1)}, u32[]{:S(2)}) copy-start(bf16[256,1,1792]{2,0,1:T(8,128)(2,1)} %copy.113) | copy-start | bytes 2752516
  112.6 7.1 %copy-start.35 = (bf16[256,1,1791]{0,2,1:T(8,128)(2,1)S(1)}, bf16[256,1,1791]{0,2,1:T(8,128)(2,1)}, u32[]{:S(2)}) copy-start(bf16[256,1,1791]{0,2,1:T(8,128)(2,1)} %get-tuple-element.12) | copy-start | bytes 2750980
  115.6 5.6 %copy-start.34 = (bf16[256,1,1791]{0,2,1:T(8,128)(2,1)S(1)}, bf16[256,1,1791]{0,2,1:T(8,128)(2,1)}, u32[]{:S(2)}) copy-start(bf16[256,1,1791]{0,2,1:T(8,128)(2,1)} %get-tuple-element.11) | copy-start | bytes 2750980
  118.6 4.2 %copy-start.10 = (bf16[256,1,1792]{2,0,1:T(8,128)(2,1)S(1)}, bf16[256,1,1792]{2,0,1:T(8,128)(2,1)}, u32[]{:S(2)}) copy-start(bf16[256,1,1792]{2,0,1:T(8,128)(2,1)} %copy.114) | copy-start | bytes 2752516
  119.7 4.2 %copy-start.29 = (bf16[256,1,1793]{0,2,1:T(8,128)(2,1)S(1)}, bf16[256,1,1793]{0,2,1:T(8,128)(2,1)}, u32[]{:S(2)}) copy-start(bf16[256,1,1793]{0,2,1:T(8,128)(2,1)} %get-tuple-element.23) | copy-start | bytes 2754052
  121.2 4.1 %copy-start.25 = (bf16[256,1,2047]{0,2,1:T(8,128)(2,1)S(1)}, bf16[256,1,2047]{0,2,1:T(8,128)(2,1)}, u32[]{:S(2)}) copy-start(bf16[256,1,2047]{0,2,1:T(8,128)(2,1)} %get-tuple-element.29) | copy-start | bytes 3144196
  132.4 6.0 %copy-start.2 = (bf16[16,8,8,256]{3,1,2,0:T(8,128)(2,1)S(1)}, bf16[16,8,8,256]{3,1,2,0:T(8,128)(2,1)}, u32[]{:S(2)}) copy-start(bf16[16,8,8,256]{3,1,2,0:T(8,128)(2,1)} %copy.118) | copy-start | bytes 1572868
  132.4 6.0 %copy-start.13 = (bf16[256,1,1792]{2,0,1:T(8,128)(2,1)S(1)}, bf16[256,1,1792]{2,0,1:T(8,128)(2,1)}, u32[]{:S(2)}) copy-start(bf16[256,1,1792]{2,0,1:T(8,128)(2,1)} %copy.115) | copy-start | bytes 2752516
  132.4 7.1 %copy-start.33 = (bf16[256,1,1791]{0,2,1:T(8,128)(2,1)S(1)}, bf16[256,1,1791]{0,2,1:T(8,128)(2,1)}, u32[]{:S(2)}) copy-start(bf16[256,1,1791]{0,2,1:T(8,128)(2,1)} %get-tuple-element.10) | copy-start | bytes 2750980
  135.4 5.6 %copy-start.32 = (bf16[256,1,1791]{0,2,1:T(8,128)(2,1)S(1)}, bf16[256,1,1791]{0,2,1:T(8,128)(2,1)}, u32[]{:S(2)}) copy-start(bf16[256,1,1791]{0,2,1:T(8,128)(2,1)} %get-tuple-element.9) | copy-start | bytes 2750980
  138.4 4.2 %copy-start.11 = (bf16[256,1,1792]{2,0,1:T(8,128)(2,1)S(1)}, bf16[256,1,1792]{2,0,1:T(8,128)(2,1)}, u32[]{:S(2)}) copy-start(bf16[256,1,1792]{2,0,1:T(8,128)(2,1)} %copy.116) | copy-start | bytes 2752516
  139.5 4.2 %copy-start.28 = (bf16[256,1,1793]{0,2,1:T(8,128)(2,1)S(1)}, bf16[256,1,1793]{0,2,1:T(8,128)(2,1)}, u32[]{:S(2)}) copy-start(bf16[256,1,1793]{0,2,1:T(8,128)(2,1)} %get-tuple-element.21) | copy-start | bytes 2754052
  141.0 4.1 %copy-start.24 = (bf16[256,1,2047]{0,2,1:T(8,128)(2,1)S(1)}, bf16[256,1,2047]{0,2,1:T(8,128)(2,1)}, u32[]{:S(2)}) copy-start(bf16[256,1,2047]{0,2,1:T(8,128)(2,1)} %get-tuple-element.27) | copy-start | bytes 3144196
  147.8 4.7 %copy-start.3 = (bf16[16,8,8,256]{3,1,2,0:T(8,128)(2,1)S(1)}, bf16[16,8,8,256]{3,1,2,0:T(8,128)(2,1)}, u32[]{:S(2)}) copy-start(bf16[16,8,8,256]{3,1,2,0:T(8,128)(2,1)} %copy.118) | copy-start | bytes 1572868
  147.8 4.7 %copy-start.27 = (bf16[256,1,1793]{0,2,1:T(8,128)(2,1)S(1)}, bf16[256,1,1793]{0,2,1:T(8,128)(2,1)}, u32[]{:S(2)}) copy-start(bf16[256,1,1793]{0,2,1:T(8,128)(2,1)} %get-tuple-element.20) | copy-start | bytes 2754052
  149.6 5.6 %copy-start.31 = (bf16[256,1,1791]{0,2,1:T(8,128)(2,1)S(1)}, bf16[256,1,1791]{0,2,1:T(8,128)(2,1)}, u32[]{:S(2)}) copy-start(bf16[256,1,1791]{0,2,1:T(8,128)(2,1)} %get-tuple-element.8) | copy-start | bytes 2750980
  154.1 2.7 copy-start.23
  155.2 2.4 copy-start.15
  155.2 2.4 copy-start.16
  156.6 3.7 %copy-start.17 = (bf16[128,1,1793]{0,2,1:T(8,128)(2,1)S(1)}, bf16[128,1,1793]{0,2,1:T(8,128)(2,1)}, u32[]{:S(2)}) copy-start(bf16[128,1,1793]{0,2,1:T(8,128)(2,1)} %get-tuple-element.49) | copy-start | bytes 1377028
  156.6 3.7 %copy-start.18 = (bf16[128,1,1793]{0,2,1:T(8,128)(2,1)S(1)}, bf16[128,1,1793]{0,2,1:T(8,128)(2,1)}, u32[]{:S(2)}) copy-start(bf16[128,1,1793]{0,2,1:T(8,128)(2,1)} %get-tuple-element.51) | copy-start | bytes 1377028
  156.7 5.2 %copy-start.22 = (bf16[128,1,1792]{0,2,1:T(8,128)(2,1)S(1)}, bf16[128,1,1792]{0,2,1:T(8,128)(2,1)}, u32[]{:S(2)}) copy-start(bf16[128,1,1792]{0,2,1:T(8,128)(2,1)} %get-tuple-element.43) | copy-start | bytes 1376260
  156.7 6.1 %copy-start.21 = (bf16[128,1,1792]{0,2,1:T(8,128)(2,1)S(1)}, bf16[128,1,1792]{0,2,1:T(8,128)(2,1)}, u32[]{:S(2)}) copy-start(bf16[128,1,1792]{0,2,1:T(8,128)(2,1)} %get-tuple-element.45) | copy-start | bytes 1376260
  156.7 145.1 %reduce-scatter.2.cloned.1.call-start = ((), (), s32[]{:S(2)}) async-start(), calls=%async_computation.1 | async-start | bytes 3145728 | tf_op jit(solution)/shard_map/reduce_scatter | solution.py:71
  157.6 6.0 %copy-start.19 = (bf16[128,1,1791]{0,2,1:T(8,128)(2,1)S(1)}, bf16[128,1,1791]{0,2,1:T(8,128)(2,1)}, u32[]{:S(2)}) copy-start(bf16[128,1,1791]{0,2,1:T(8,128)(2,1)} %get-tuple-element.37) | copy-start | bytes 1375492
  157.6 6.0 %copy-start.20 = (bf16[128,1,1791]{0,2,1:T(8,128)(2,1)S(1)}, bf16[128,1,1791]{0,2,1:T(8,128)(2,1)}, u32[]{:S(2)}) copy-start(bf16[128,1,1791]{0,2,1:T(8,128)(2,1)} %get-tuple-element.39) | copy-start | bytes 1375492
  178.5 6.9 %copy-start.38 = (bf16[256,9,128]{0,2,1:T(8,128)(2,1)S(1)}, bf16[256,9,128]{0,2,1:T(8,128)(2,1)}, u32[]{:S(2)}) copy-start(bf16[256,9,128]{0,2,1:T(8,128)(2,1)} %get-tuple-element.34) | copy-start | bytes 1769476
  178.5 11.1 %slice-start = ((s8[4718592]{0:T(1024)(128)(4,1)}), s8[524288]{0:T(1024)(128)(4,1)S(1)}, s32[]{:S(2)}) async-start(s8[4718592]{0:T(1024)(128)(4,1)} %bitcast.360), calls=%async_computation.3 | async-start | bytes 1048576
  185.4 4.2 %slice-start.1 = ((s8[4718592]{0:T(1024)(128)(4,1)}), s8[4194304]{0:T(1024)(128)(4,1)S(1)}, s32[]{:S(2)}) async-start(s8[4718592]{0:T(1024)(128)(4,1)} %bitcast.360), calls=%async_computation.4 | async-start | bytes 8388608
  185.4 4.2 %copy-start.37 = (bf16[256,9,128]{0,2,1:T(8,128)(2,1)S(1)}, bf16[256,9,128]{0,2,1:T(8,128)(2,1)}, u32[]{:S(2)}) copy-start(bf16[256,9,128]{0,2,1:T(8,128)(2,1)} %get-tuple-element.33) | copy-start | bytes 1769476
  189.6 2.4 copy-start.7
  189.6 2.6 copy-start.36
Sparse Core Ops, SparseCore 0:
  156.8 140.7 all-reduce.49
Sparse Core Ops, SparseCore 1:
  195.3 10.7 reduce-scatter.1
where the time goes:
time: 313 us; the launch traced here: 312 us
  waiting for transfers between devices  141 us (45%)
  local copies, waits for them, and re-layouts  65.7 us (21%)
  matrix products  56.2 us (18%)
  other arithmetic  18.9 us (6%)
  between operations  15.8 us (5%)
  starting transfers between devices  14.6 us (5%)
    psum x1, waiting for transfers between devices, local(): weight_grad = lax.psum(local_grad, 'gy') * norm_factor  102 us
    dot_general x27, matrix products, local(): lax.dot_general(moved, grad_flat, (((1,), (1,)), ((), ())), preferred_ele...  47.3 us
    ppermute x2, waiting for transfers between devices, padded(): lax.ppermute(lax.slice_in_dim(block, block.shape[dim] - width, None, axis...  38.2 us
    unnamed x99, local copies, waits for them, and re-layouts  28.2 us
    another operation x3, local copies, waits for them, and re-layouts, grad_group(): stacked = jnp.stack(pieces_list, 0)  20.2 us
    ppermute x2, starting transfers between devices, padded(): lax.ppermute(lax.slice_in_dim(block, block.shape[dim] - width, None, axis...  12 us
    slice x4, local copies, waits for them, and re-layouts, shift_cells(): moved = jnp.concatenate([flat[..., -offset:], filler], axis=-1)  10.8 us
    dot_general x3, matrix products, local(): jnp.dot(tap_cols, stacks[partial_y_off], preferred_element_type=jnp.float32)  8.93 us
  transfers between devices with their start and end apart: 6, of which 3 were waited for; matrix products, arithmetic and copies ran while one was open for 19% of the time, Pallas kernels for 0%

commit v1 on v0

--- a/solution.py
+++ b/solution.py
@@ -3,6 +3,7 @@
 import jax.numpy as jnp
 from jax import lax
 from jax.sharding import PartitionSpec as P
+from jax.lax import all_gather
 
 
 def padded(block, sides, width):
@@ -91,7 +92,10 @@
                 )
     local_grad = jnp.stack(tap_grads, 0)
     norm_factor = 1.0 / math.sqrt(row_count * lax.axis_size("gy") * z_count * x_count)
-    weight_grad = lax.psum(local_grad, "gy") * norm_factor
+    supply_all_the_modes = lambda t0, chip_axis: jnp.sum(
+        all_gather(t0, axis_name=chip_axis), axis=0
+    )
+    weight_grad = supply_all_the_modes(local_grad, "gy") * norm_factor
     return (input_grad, weight_grad)
 
 

time: 313 us -> 749 us (2.39)
  waiting for transfers between devices: 141 us -> 569 us
  other arithmetic: 18.9 us -> 32.6 us
    all_gather x0 -> x1, waiting for transfers between devices: none -> 538 us  [local(): all_gather(t0, axis_name=chip_axis)]
    psum x1 -> x0, waiting for transfers between devices: 102 us -> none  [local(): weight_grad = lax.psum(local_grad, 'gy') * norm_factor]
    reduce_sum x0 -> x1, other arithmetic: none -> 11.8 us  [local(): jnp.sum(all_gather(t0, axis_name=chip_axis), axis=0)]
    ppermute x2, waiting for transfers between devices: 38.2 us -> 30.1 us  [padded(): lax.ppermute(lax.slice_in_dim(block, block.shape[dim] - width, None, axis...]
    unnamed x99 -> x73, local copies, waits for them, and re-layouts: 28.2 us -> 28.3 us
  transfers between devices with their start and end apart: 6 -> 6, of which waited for: 3 -> 2; matrix products, arithmetic and copies ran while one was open for 19% -> 18% of each run, Pallas kernels for 0% -> 0%
where the time goes in v1:
time: 749 us; the launch traced here: 748 us
  waiting for transfers between devices  569 us (76%)
  local copies, waits for them, and re-layouts  62.1 us (8%)
  matrix products  54.6 us (7%)
  other arithmetic  32.6 us (4%)
  between operations  15.7 us (2%)
  starting transfers between devices  14.6 us (2%)
    all_gather x1, waiting for transfers between devices, local(): all_gather(t0, axis_name=chip_axis)  538 us
    dot_general x27, matrix products, local(): lax.dot_general(moved, grad_flat, (((1,), (1,)), ((), ())), preferred_ele...  45.7 us
    ppermute x2, waiting for transfers between devices, padded(): lax.ppermute(lax.slice_in_dim(block, block.shape[dim] - width, None, axis...  30.1 us
    unnamed x73, local copies, waits for them, and re-layouts  28.3 us
    another operation x3, local copies, waits for them, and re-layouts, grad_group(): stacked = jnp.stack(pieces_list, 0)  20.3 us
  transfers between devices with their start and end apart: 6, of which 2 were waited for; matrix products, arithmetic and copies ran while one was open for 18% of the time, Pallas kernels for 0%

profile of v1, /device:TPU:0, one launch (start us, length us, event | category | flops | bytes accessed | tf_op | source)
XLA Modules:
  0.0 748.3 jit_solution(11213918341136960621)
XLA Ops:
  8.1 2.3 copy.111
  11.6 6.3 collective-permute-start
  17.9 1.6 copy.120
  20.9 5.7 collective-permute-start.2
  26.5 2.6 copy.115
  31.3 30.1 %collective-permute-done = bf16[128,1,8,256]{0,3,2,1:T(8,128)(2,1)} collective-permute-done((bf16[128,1,8,256]{0,3,2,1:T(8,128)(2,1)}, bf16[128,1,8,256]{0,3,2,1:T(8,128)(2,1)}, u32[]{:S(2)}, u32[]{:S(2)}) %collective-permute-start) | collective-permute-done | bytes 524320 | tf_op jit(solution)/shard_map/ppermute | solution.py:14
  61.4 1.5 pad_maximum_fusion.1
  68.4 1.6 bitcast_dynamic-update-slice_fusion.4
  77.4 1.8 bitcast_dynamic-update-slice_fusion
  79.2 1.5 bitcast_dynamic-update-slice_fusion.10
  82.5 1.5 bitcast_dynamic-update-slice_fusion.8
  84.0 6.7 copy.114
  90.7 6.7 copy.116
  97.4 6.9 copy.119
  104.3 4.1 fusion.165
  108.5 1.7 convolution_add_fusion.1
  110.8 3.1 fusion
  114.0 2.2 pad_maximum_fusion
  116.2 2.6 fusion.156
  118.8 2.5 fusion.157
  121.3 2.6 fusion.158
  124.0 2.9 fusion.159
  126.8 2.2 copy.152
  129.1 3.0 fusion.27
  132.1 2.4 fusion.26
  134.5 1.5 fusion.25
  136.0 1.5 fusion.24
  138.6 2.2 copy.153
  140.8 3.0 fusion.22
  143.9 3.0 fusion.21
  149.4 1.5 fusion.18
  150.9 2.2 copy.154
  153.2 2.2 copy.155
  155.4 2.2 copy.156
  157.6 2.2 copy.157
  159.8 2.5 fusion.17
  162.3 2.9 fusion.16
  165.2 1.5 fusion.15
  167.9 1.5 fusion.13
  169.4 1.5 fusion.12
  172.1 1.5 fusion.10
  173.6 1.5 fusion.9
  177.7 1.5 fusion.6
  180.4 1.5 fusion.4
  181.9 1.6 fusion.3
  188.5 538.4 %all-gather.3.cloned.1.call-done = f32[216,256,128]{2,1,0:T(8,128)} async-done(((f32[27,256,128]{2,1,0:T(8,128)}), f32[216,256,128]{2,1,0:T(8,128)}) %all-gather.3.cloned.1.call-update) | async-done | bytes 28311568 | tf_op jit(solution)/shard_map/all_gather | solution.py:96
  727.0 11.8 %reduce_sum.9 = f32[27,256,128]{2,1,0:T(8,128)S(1)} reduce(f32[8,27,256,128]{3,2,1,0:T(8,128)} %bitcast.331, f32[]{:T(128)} %constant.141.clone.1), dimensions={0}, to_apply=%region_1.2 | reduce | flops 6193152 | bytes 31850500 | tf_op jit(solution)/shard_map/reduce_sum | solution.py:95
  738.8 2.0 broadcast_multiply_fusion
  (99 shorter events, 34.8 us)
Async XLA Ops:
  8.0 21.2 %copy-start.9 = (bf16[128,1,8,256]{3,2,1,0:T(8,128)(2,1)S(1)}, bf16[128,1,8,256]{3,2,1,0:T(8,128)(2,1)}, u32[]{:S(2)}) copy-start(bf16[128,1,8,256]{3,2,1,0:T(8,128)(2,1)} %param.4) | copy-start | bytes 1572868
  8.0 178.0 %reduce-scatter.2.cloned.1.call-start = ((), (), s32[]{:S(2)}) async-start(), calls=%async_computation.1 | async-start | bytes 3145728 | tf_op jit(solution)/shard_map/reduce_scatter | solution.py:72
  10.3 21.0 %collective-permute-start.1 = (bf16[128,1,8,256]{0,3,2,1:T(8,128)(2,1)}, bf16[128,1,8,256]{0,3,2,1:T(8,128)(2,1)}, u32[]{:S(2)}, u32[]{:S(2)}) collective-permute-start(bf16[128,1,8,256]{0,3,2,1:T(8,128)(2,1)} %copy.111), channel_id=1, source_target_pairs={{2,0},{4,2},{6,4},{8,6},{10,8},{12,10},{14,12},{3,1},{5,3},{7,5},{... | collective-permute-start | bytes 1572872 | tf_op jit(solution)/shard_map/ppermute | solution.py:17
  11.6 49.8 %collective-permute-start = (bf16[128,1,8,256]{0,3,2,1:T(8,128)(2,1)}, bf16[128,1,8,256]{0,3,2,1:T(8,128)(2,1)}, u32[]{:S(2)}, u32[]{:S(2)}) collective-permute-start(bf16[128,1,8,256]{0,3,2,1:T(8,128)(2,1)} %copy.111), channel_id=1, source_target_pairs={{0,2},{2,4},{4,6},{6,8},{8,10},{10,12},{12,14},{1,3},{3,5},{5,7},{... | collective-permute-start | bytes 1572872 | tf_op jit(solution)/shard_map/ppermute | solution.py:14
  19.6 11.7 %copy-start.4 = (bf16[256,1,8,256]{0,3,2,1:T(8,128)(2,1)}, bf16[256,1,8,256]{0,3,2,1:T(8,128)(2,1)S(1)}, u32[]{:S(2)}) copy-start(bf16[256,1,8,256]{0,3,2,1:T(8,128)(2,1)S(1)} %copy.120) | copy-start | bytes 3145732
  19.6 94.4 %collective-permute-start.3 = (bf16[256,1,8,256]{0,3,2,1:T(8,128)(2,1)S(1)}, bf16[256,1,8,256]{0,3,2,1:T(8,128)(2,1)}, u32[]{:S(2)}, u32[]{:S(2)}) collective-permute-start(bf16[256,1,8,256]{0,3,2,1:T(8,128)(2,1)S(1)} %copy.120), channel_id=1, source_target_pairs={{2,0},{4,2},{6,4},{8,6},{10,8},{12,10},{14,12},{3,1},{5,3},{7,5},{... | collective-permute-start | bytes 3145736 | tf_op jit(solution)/shard_map/ppermute | solution.py:17
  20.9 93.1 %collective-permute-start.2 = (bf16[256,1,8,256]{0,3,2,1:T(8,128)(2,1)S(1)}, bf16[256,1,8,256]{0,3,2,1:T(8,128)(2,1)}, u32[]{:S(2)}, u32[]{:S(2)}) collective-permute-start(bf16[256,1,8,256]{0,3,2,1:T(8,128)(2,1)S(1)} %copy.120), channel_id=1, source_target_pairs={{0,2},{2,4},{4,6},{6,8},{8,10},{10,12},{12,14},{1,3},{3,5},{5,7},{... | collective-permute-start | bytes 3145736 | tf_op jit(solution)/shard_map/ppermute | solution.py:14
  97.4 6.9 copy-start.25
  97.4 11.0 %slice-start = ((s8[4718592]{0:T(1024)(128)(4,1)}), s8[524288]{0:T(1024)(128)(4,1)S(1)}, s32[]{:S(2)}) async-start(s8[4718592]{0:T(1024)(128)(4,1)} %bitcast.362), calls=%async_computation.3 | async-start | bytes 1048576
  104.3 4.1 slice-start.1
  104.3 4.1 copy-start.24
  108.5 2.3 copy-start.3
  113.9 613.1 %all-gather.3.cloned.1.call-start = ((), (), s32[]{:S(2)}) async-start(), calls=%async_computation.2 | async-start | bytes 31850496 | tf_op jit(solution)/shard_map/all_gather | solution.py:96
  129.1 5.4 copy-start
  129.1 5.4 copy-start.18
  129.1 6.9 copy-start.14
  140.8 6.0 copy-start.1
  140.8 6.0 copy-start.8
  140.8 7.1 copy-start.23
  143.9 5.5 copy-start.22
  159.8 5.4 copy-start.2
  159.8 5.4 copy-start.13
  162.3 5.6 copy-start.12
  165.2 4.2 copy-start.17
  166.8 4.2 copy-start.7
  167.9 4.2 copy-start.21
  169.4 4.2 copy-start.20
  171.0 4.1 copy-start.6
  172.1 4.2 copy-start.16
  173.6 4.1 copy-start.11
  176.2 4.2 copy-start.10
  177.7 4.2 copy-start.15
  179.2 4.2 copy-start.5
  180.4 4.2 copy-start.19
Sparse Core Ops, SparseCore 0:
  114.0 11.0 reduce-scatter.1
Sparse Core Ops, SparseCore 1:
  186.1 540.8 all-gather.2
